TPU v7x, 32 devices: a whole 2x2x4 slice. The times are simulated.
32 devices in a mesh: seg: 4 (over x, core), blk: 8 (over z, y).
Axes of the slice: x: 2, y: 2, z: 4, core: 2. Of those that a mesh axis runs over, the one named last changes fastest.
Arguments:
- start_state: float32 [32, 256, 256], P(('seg', 'blk')), may hold values from -6 to 6
- sector_sizes: int32 [32], P(('seg', 'blk')), may hold values from 128 to 256, as said below
- partner: int32 [32, 16], P(('seg', 'blk')), may hold values from 0 to 7
- left_diag: bfloat16 [32, 256, 256], P(('seg', 'blk')), may hold values from -2 to 4, as said below
- right_diag: bfloat16 [32, 256, 256], P(('seg', 'blk')), may hold values from -2 to 4, as said below
- left_hop: bfloat16 [32, 16, 256, 256], P(('seg', 'blk')), may hold values from -0.375 to 0.375
- right_hop: bfloat16 [32, 16, 256, 256], P(('seg', 'blk')), may hold values from -0.375 to 0.375
- left_coupling: float32 [4, 17], P('seg'), may hold values from 0.3 to 3
- right_coupling: float32 [4, 17], P('seg'), may hold values from 0.3 to 3
Outputs:
- state: float32 [32, 256, 256], P(('seg', 'blk'))
- energy: float32 [4], P('seg')
- left_boundary: bfloat16 [32, 256, 256], P(('seg', 'blk'))
- right_boundary: bfloat16 [32, 256, 256], P(('seg', 'blk'))
Inputs may be any that keep to these rules, and one draw needn't show every extreme that they name: `sector_sizes`: in every segment one sector has exactly 256 live states and another exactly 128. `left_diag`: symmetric blocks with diagonal entries from 1 to 4. `right_diag`: symmetric blocks with diagonal entries from 1 to 4.
All inputs are finite; a program needn't handle non-finite values.
Results may differ from a plain program's by a relative error of at most 0.017.
Values may be sent and summed in bfloat16 or wider, within the bound.
A program may use at most 64 MiB of HBM per device.

v0:
```python
import math

import jax
import jax.numpy as jnp
from jax import lax
from jax.sharding import PartitionSpec as P

ITERS = 4


EPS = 1e-06


def passed_along(value, axis, steps):
    count = lax.axis_size(axis)
    first, last = (max(0, -steps), min(count, count - steps))
    return lax.ppermute(value, axis, [(source, source + steps) for source in range(first, last)])


def rotate(rayleigh, coupling, curvature):
    half = 0.5 * (curvature - rayleigh)
    radius = jnp.sqrt(half * half + coupling * coupling)
    lowest = 0.5 * (rayleigh + curvature) - radius
    return (radius + half, -coupling, lowest)


def total(first, second):
    return jnp.sum(first * second)


def on_device(
    start_state,
    sector_sizes,
    partner,
    left_diag,
    right_diag,
    left_hop,
    right_hop,
    left_coupling,
    right_coupling,
):
    count, width, _ = start_state.shape
    sectors = count * lax.axis_size("blk")
    index = jnp.arange(width)
    live = (index[None, :, None] < sector_sizes[:, None, None]) & (
        index[None, None, :] < sector_sizes[:, None, None]
    )
    mask = live.astype(jnp.float32)
    hdiag = (
        jnp.diagonal(left_diag, axis1=1, axis2=2).astype(jnp.float32)[:, :, None]
        + jnp.diagonal(right_diag, axis1=1, axis2=2).astype(jnp.float32)[:, None, :]
    )

    def apply(field):
        rounded = field.astype(jnp.bfloat16)
        whole = lax.all_gather(rounded, "blk", axis=0, tiled=True)
        own = jnp.einsum("qij,qjk->qik", left_diag, rounded, preferred_element_type=jnp.float32)
        own = own + jnp.einsum(
            "qij,qjk->qik", rounded, right_diag, preferred_element_type=jnp.float32
        )
        source = whole[partner]
        middle = jnp.einsum(
            "qkij,qkjl->qkil", left_hop, source, preferred_element_type=jnp.float32
        ).astype(jnp.bfloat16)
        hop = jnp.einsum("qkij,qkjl->qil", middle, right_hop, preferred_element_type=jnp.float32)
        return (own + hop) * mask

    state = start_state * mask
    state = state * lax.rsqrt(lax.psum(total(state, state), "blk") + EPS)
    image = apply(state)
    lowest = jnp.float32(0.0)
    for step in range(ITERS):
        rayleigh = lax.psum(total(state, image), "blk")
        correction = (image - rayleigh * state) / hdiag
        correlation = lax.psum(total(state, correction), "blk")
        correction = correction - correlation * state
        spread = lax.psum(total(correction, correction), "blk")
        direction = correction * lax.rsqrt(spread + EPS)
        pushed = apply(direction)
        coupling, curvature = lax.psum((total(state, pushed), total(direction, pushed)), "blk")
        alpha, beta, lowest = rotate(rayleigh, coupling, curvature)
        state = alpha * state + beta * direction
        image = alpha * image + beta * pushed
        newsq = lax.psum(total(state, state), "blk")
        scale = lax.rsqrt(newsq + EPS)
        state = state * scale
        image = image * scale
    scaled = (state * (width * math.sqrt(sectors))).astype(jnp.bfloat16)
    left_ops = jnp.concatenate([left_diag[:, None], left_hop], axis=1)
    right_ops = jnp.concatenate([right_diag[:, None], right_hop], axis=1)
    left_mid = jnp.einsum(
        "qcij,qjb->qcib", left_ops, scaled, preferred_element_type=jnp.float32
    ).astype(jnp.bfloat16)
    left_env = (
        jnp.einsum("qia,qcib->qcab", scaled, left_mid, preferred_element_type=jnp.float32) / width
    ).astype(jnp.bfloat16)
    right_mid = jnp.einsum(
        "qai,qcij->qcaj", scaled, right_ops, preferred_element_type=jnp.float32
    ).astype(jnp.bfloat16)
    right_env = (
        jnp.einsum("qcaj,qbj->qcab", right_mid, scaled, preferred_element_type=jnp.float32) / width
    ).astype(jnp.bfloat16)
    left_arrived = passed_along(left_env, "seg", 1)
    right_arrived = passed_along(right_env, "seg", -1)
    left_boundary = jnp.einsum(
        "c,qcab->qab", left_coupling[0], left_arrived.astype(jnp.float32)
    ).astype(jnp.bfloat16)
    right_boundary = jnp.einsum(
        "c,qcab->qab", right_coupling[0], right_arrived.astype(jnp.float32)
    ).astype(jnp.bfloat16)
    return (state, jnp.reshape(lowest, (1,)), left_boundary, right_boundary)


def solution(mesh):
    placed = (
        P(("seg", "blk"), None, None),
        P(("seg", "blk")),
        P(("seg", "blk"), None),
        P(("seg", "blk"), None, None),
        P(("seg", "blk"), None, None),
        P(("seg", "blk"), None, None, None),
        P(("seg", "blk"), None, None, None),
        P("seg", None),
        P("seg", None),
    )
    return jax.shard_map(
        on_device,
        mesh=mesh,
        in_specs=placed,
        out_specs=(
            P(("seg", "blk"), None, None),
            P("seg"),
            P(("seg", "blk"), None, None),
            P(("seg", "blk"), None, None),
        ),
        check_vma=False,
    )
```

profile of v0, /device:TPU:1, one launch (start us, length us, event | category | flops | bytes accessed | tf_op | source)
XLA Modules:
  0.0 750.2 jit_solution(5439851372307914648)
XLA Ops:
  9.8 19.4 %psum.175 = f32[]{:T(128)} all-reduce(f32[]{:T(128)} %multiply_reduce_fusion.14), channel_id=1, replica_groups=mesh['seg'=4,'blk'=8] {'blk'}, use_global_device_ids=true, to_apply=%region_1.2 | all-reduce | flops 1 | bytes 8 | tf_op jit(solution)/shard_map/psum | solution.py:69
  30.8 2.6 gather_fusion.1
  33.5 2.5 gather_fusion.2
  36.3 34.8 %all-gather.6.cloned.1.call-done = bf16[8,256,256]{2,1,0:T(8,128)(2,1)} async-done(((bf16[1,256,256]{2,1,0:T(8,128)(2,1)}), bf16[8,256,256]{2,1,0:T(8,128)(2,1)}) %all-gather.6.cloned.1.call-update) | async-done | bytes 1048592 | tf_op jit(solution)/shard_map/all_gather | solution.py:56
  71.1 3.3 gather_fusion
  74.3 4.7 fusion.80
  79.0 1.8 fusion.124
  80.9 15.2 %psum.176 = f32[]{:T(128)} all-reduce(f32[]{:T(128)} %get-tuple-element.52), channel_id=1, replica_groups=mesh['seg'=4,'blk'=8] {'blk'}, use_global_device_ids=true, to_apply=%region_3.4 | all-reduce | flops 1 | bytes 8 | tf_op jit(solution)/shard_map/psum | solution.py:73
  96.1 1.4 multiply_reduce_fusion.13
  97.6 14.8 %psum.177 = f32[]{:T(128)} all-reduce(f32[]{:T(128)} %multiply_reduce_fusion.13), channel_id=1, replica_groups=mesh['seg'=4,'blk'=8] {'blk'}, use_global_device_ids=true, to_apply=%region_5.6 | all-reduce | flops 1 | bytes 8 | tf_op jit(solution)/shard_map/psum | solution.py:75
  112.4 2.1 multiply_reduce_fusion.12
  114.5 15.4 %psum.178 = f32[]{:T(128)} all-reduce(f32[]{:T(128)} %get-tuple-element.50), channel_id=1, replica_groups=mesh['seg'=4,'blk'=8] {'blk'}, use_global_device_ids=true, to_apply=%region_7.8 | all-reduce | flops 1 | bytes 8 | tf_op jit(solution)/shard_map/psum | solution.py:77
  132.4 48.4 %all-gather.8.cloned.1.call-done = bf16[8,256,256]{2,1,0:T(8,128)(2,1)} async-done(((bf16[1,256,256]{2,1,0:T(8,128)(2,1)}), bf16[8,256,256]{2,1,0:T(8,128)(2,1)}) %all-gather.8.cloned.1.call-update) | async-done | bytes 1048592 | tf_op jit(solution)/shard_map/all_gather | solution.py:56
  180.8 3.3 gather_fusion.3
  184.0 4.7 fusion.87
  188.7 2.6 fusion.122
  191.3 15.2 %all-reduce.3 = (f32[]{:T(128)}, f32[]{:T(128)}) all-reduce(f32[]{:T(128)} %get-tuple-element.23, f32[]{:T(128)} %get-tuple-element.22), channel_id=1, replica_groups=mesh['seg'=4,'blk'=8] {'blk'}, use_global_device_ids=true, to_apply=%region_11.12 | all-reduce | flops 2 | bytes 16 | tf_op jit(solution)/shard_map/psum | solution.py:80
  210.6 14.8 %psum.181 = f32[]{:T(128)} all-reduce(f32[]{:T(128)} %get-tuple-element.48), channel_id=1, replica_groups=mesh['seg'=4,'blk'=8] {'blk'}, use_global_device_ids=true, to_apply=%region_13.14 | all-reduce | flops 1 | bytes 8 | tf_op jit(solution)/shard_map/psum | solution.py:84
  226.2 1.6 fusion.121
  227.8 15.4 %psum.182 = f32[]{:T(128)} all-reduce(f32[]{:T(128)} %get-tuple-element.46), channel_id=1, replica_groups=mesh['seg'=4,'blk'=8] {'blk'}, use_global_device_ids=true, to_apply=%region_15.16 | all-reduce | flops 1 | bytes 8 | tf_op jit(solution)/shard_map/psum | solution.py:73
  243.2 1.4 multiply_reduce_fusion.10
  244.6 14.6 %psum.183 = f32[]{:T(128)} all-reduce(f32[]{:T(128)} %multiply_reduce_fusion.10), channel_id=1, replica_groups=mesh['seg'=4,'blk'=8] {'blk'}, use_global_device_ids=true, to_apply=%region_17.18 | all-reduce | flops 1 | bytes 8 | tf_op jit(solution)/shard_map/psum | solution.py:75
  259.2 2.1 multiply_reduce_fusion.9
  261.2 15.4 %psum.184 = f32[]{:T(128)} all-reduce(f32[]{:T(128)} %get-tuple-element.44), channel_id=1, replica_groups=mesh['seg'=4,'blk'=8] {'blk'}, use_global_device_ids=true, to_apply=%region_19.20 | all-reduce | flops 1 | bytes 8 | tf_op jit(solution)/shard_map/psum | solution.py:77
  279.1 55.9 %all-gather.10.cloned.1.call-done = bf16[8,256,256]{2,1,0:T(8,128)(2,1)} async-done(((bf16[1,256,256]{2,1,0:T(8,128)(2,1)}), bf16[8,256,256]{2,1,0:T(8,128)(2,1)}) %all-gather.10.cloned.1.call-update) | async-done | bytes 1048592 | tf_op jit(solution)/shard_map/all_gather | solution.py:56
  335.0 3.3 gather_fusion.4
  338.3 4.7 fusion.94
  343.0 2.6 fusion.119
  345.6 15.2 %all-reduce.2 = (f32[]{:T(128)}, f32[]{:T(128)}) all-reduce(f32[]{:T(128)} %get-tuple-element.21, f32[]{:T(128)} %get-tuple-element.20), channel_id=1, replica_groups=mesh['seg'=4,'blk'=8] {'blk'}, use_global_device_ids=true, to_apply=%region_23.24 | all-reduce | flops 2 | bytes 16 | tf_op jit(solution)/shard_map/psum | solution.py:80
  364.8 14.8 %psum.187 = f32[]{:T(128)} all-reduce(f32[]{:T(128)} %get-tuple-element.42), channel_id=1, replica_groups=mesh['seg'=4,'blk'=8] {'blk'}, use_global_device_ids=true, to_apply=%region_25.26 | all-reduce | flops 1 | bytes 8 | tf_op jit(solution)/shard_map/psum | solution.py:84
  380.3 1.6 fusion.118
  381.9 15.4 %psum.188 = f32[]{:T(128)} all-reduce(f32[]{:T(128)} %get-tuple-element.40), channel_id=1, replica_groups=mesh['seg'=4,'blk'=8] {'blk'}, use_global_device_ids=true, to_apply=%region_27.28 | all-reduce | flops 1 | bytes 8 | tf_op jit(solution)/shard_map/psum | solution.py:73
  397.4 1.4 multiply_reduce_fusion.7
  398.8 14.6 %psum.189 = f32[]{:T(128)} all-reduce(f32[]{:T(128)} %multiply_reduce_fusion.7), channel_id=1, replica_groups=mesh['seg'=4,'blk'=8] {'blk'}, use_global_device_ids=true, to_apply=%region_29.30 | all-reduce | flops 1 | bytes 8 | tf_op jit(solution)/shard_map/psum | solution.py:75
  413.3 2.1 multiply_reduce_fusion.6
  415.4 15.4 %psum.190 = f32[]{:T(128)} all-reduce(f32[]{:T(128)} %get-tuple-element.38), channel_id=1, replica_groups=mesh['seg'=4,'blk'=8] {'blk'}, use_global_device_ids=true, to_apply=%region_31.32 | all-reduce | flops 1 | bytes 8 | tf_op jit(solution)/shard_map/psum | solution.py:77
  433.5 55.7 %all-gather.12.cloned.1.call-done = bf16[8,256,256]{2,1,0:T(8,128)(2,1)} async-done(((bf16[1,256,256]{2,1,0:T(8,128)(2,1)}), bf16[8,256,256]{2,1,0:T(8,128)(2,1)}) %all-gather.12.cloned.1.call-update) | async-done | bytes 1048592 | tf_op jit(solution)/shard_map/all_gather | solution.py:56
  489.2 3.3 gather_fusion.5
  492.4 4.7 fusion.101
  497.1 2.6 fusion.116
  499.7 15.2 %all-reduce.1 = (f32[]{:T(128)}, f32[]{:T(128)}) all-reduce(f32[]{:T(128)} %get-tuple-element.19, f32[]{:T(128)} %get-tuple-element.18), channel_id=1, replica_groups=mesh['seg'=4,'blk'=8] {'blk'}, use_global_device_ids=true, to_apply=%region_35.36 | all-reduce | flops 2 | bytes 16 | tf_op jit(solution)/shard_map/psum | solution.py:80
  518.9 14.8 %psum.193 = f32[]{:T(128)} all-reduce(f32[]{:T(128)} %get-tuple-element.36), channel_id=1, replica_groups=mesh['seg'=4,'blk'=8] {'blk'}, use_global_device_ids=true, to_apply=%region_37.38 | all-reduce | flops 1 | bytes 8 | tf_op jit(solution)/shard_map/psum | solution.py:84
  534.5 1.6 fusion.115
  536.1 15.4 %psum.194 = f32[]{:T(128)} all-reduce(f32[]{:T(128)} %get-tuple-element.34), channel_id=1, replica_groups=mesh['seg'=4,'blk'=8] {'blk'}, use_global_device_ids=true, to_apply=%region_39.40 | all-reduce | flops 1 | bytes 8 | tf_op jit(solution)/shard_map/psum | solution.py:73
  551.5 1.4 multiply_reduce_fusion.4
  552.9 14.6 %psum.195 = f32[]{:T(128)} all-reduce(f32[]{:T(128)} %multiply_reduce_fusion.4), channel_id=1, replica_groups=mesh['seg'=4,'blk'=8] {'blk'}, use_global_device_ids=true, to_apply=%region_41.42 | all-reduce | flops 1 | bytes 8 | tf_op jit(solution)/shard_map/psum | solution.py:75
  567.5 2.1 multiply_reduce_fusion.3
  569.5 15.4 %psum.196 = f32[]{:T(128)} all-reduce(f32[]{:T(128)} %get-tuple-element.32), channel_id=1, replica_groups=mesh['seg'=4,'blk'=8] {'blk'}, use_global_device_ids=true, to_apply=%region_43.44 | all-reduce | flops 1 | bytes 8 | tf_op jit(solution)/shard_map/psum | solution.py:77
  586.4 2.4 copy.79
  589.0 54.3 %all-gather.14.cloned.1.call-done = bf16[8,256,256]{2,1,0:T(8,128)(2,1)} async-done(((bf16[1,256,256]{2,1,0:T(8,128)(2,1)}), bf16[8,256,256]{2,1,0:T(8,128)(2,1)}) %all-gather.14.cloned.1.call-update) | async-done | bytes 1048592 | tf_op jit(solution)/shard_map/all_gather | solution.py:56
  643.3 3.3 gather_fusion.6
  646.6 4.7 fusion.108
  651.3 1.8 multiply_reduce_fusion.2
  653.1 15.2 %all-reduce = (f32[]{:T(128)}, f32[]{:T(128)}) all-reduce(f32[]{:T(128)} %get-tuple-element.17, f32[]{:T(128)} %get-tuple-element.16), channel_id=1, replica_groups=mesh['seg'=4,'blk'=8] {'blk'}, use_global_device_ids=true, to_apply=%region_47.48 | all-reduce | flops 2 | bytes 16 | tf_op jit(solution)/shard_map/psum | solution.py:80
  672.4 14.9 %psum.199 = f32[]{:T(128)} all-reduce(f32[]{:T(128)} %multiply_reduce_fusion), channel_id=1, replica_groups=mesh['seg'=4,'blk'=8] {'blk'}, use_global_device_ids=true, to_apply=%region_49.50 | all-reduce | flops 1 | bytes 8 | tf_op jit(solution)/shard_map/psum | solution.py:84
  688.0 4.5 fusion.2
  692.6 12.1 %collective-permute-start = (bf16[1,17,256,256]{2,3,1,0:T(8,128)(2,1)}, bf16[1,17,256,256]{2,3,1,0:T(8,128)(2,1)S(1)}, u32[]{:S(2)}, u32[]{:S(2)}) collective-permute-start(bf16[1,17,256,256]{2,3,1,0:T(8,128)(2,1)} %fusion.2), channel_id=1, source_target_pairs={{0,8},{8,16},{16,24},{1,9},{9,17},{17,25},{2,10},{10,18},{18,26},{... | collective-permute-start | bytes 6684680 | tf_op jit(solution)/shard_map/ppermute | solution.py:17
  704.7 5.1 fusion.3
  709.8 2.1 collective-permute-start.1
  714.1 15.3 %collective-permute-done = bf16[1,17,256,256]{2,3,1,0:T(8,128)(2,1)S(1)} collective-permute-done((bf16[1,17,256,256]{2,3,1,0:T(8,128)(2,1)}, bf16[1,17,256,256]{2,3,1,0:T(8,128)(2,1)S(1)}, u32[]{:S(2)}, u32[]{:S(2)}) %collective-permute-start) | collective-permute-done | bytes 2228256 | tf_op jit(solution)/shard_map/ppermute | solution.py:17
  729.4 1.4 copy-done.3
  730.8 3.7 copy.107
  735.7 3.1 collective-permute-done.1
  738.9 3.0 fusion
  (56 shorter events, 15.3 us)
Async XLA Ops:
  7.2 727.3 %copy-start = (f32[1,17]{1,0:T(1,128)S(1)}, f32[1,17]{1,0:T(1,128)}, u32[]{:S(2)}) copy-start(f32[1,17]{1,0:T(1,128)} %param.16) | copy-start | bytes 208
  7.2 28.8 %copy-start.2 = (bf16[1,256,256]{2,1,0:T(8,128)(2,1)S(1)}, bf16[1,256,256]{2,1,0:T(8,128)(2,1)}, u32[]{:S(2)}) copy-start(bf16[1,256,256]{2,1,0:T(8,128)(2,1)} %param.12) | copy-start | bytes 393220
  7.2 26.3 %copy-start.1 = (bf16[1,256,256]{2,1,0:T(8,128)(2,1)S(1)}, bf16[1,256,256]{2,1,0:T(8,128)(2,1)}, u32[]{:S(2)}) copy-start(bf16[1,256,256]{2,1,0:T(8,128)(2,1)} %param.13) | copy-start | bytes 393220
  7.2 28.8 %copy-start.5 = (s32[1,16]{1,0:T(1,128)S(1)}, s32[1,16]{1,0:T(1,128)}, u32[]{:S(2)}) copy-start(s32[1,16]{1,0:T(1,128)} %param.11) | copy-start | bytes 196
  7.2 63.9 %all-gather.6.cloned.1.call-start = ((), (), s32[]{:S(2)}) async-start(), calls=%async_computation | async-start | bytes 1179648 | tf_op jit(solution)/shard_map/all_gather | solution.py:56
  30.8 150.0 %all-gather.8.cloned.1.call-start = ((), (), s32[]{:S(2)}) async-start(), calls=%async_computation.1 | async-start | bytes 1179648 | tf_op jit(solution)/shard_map/all_gather | solution.py:56
  36.2 38.1 %copy-start.4 = (bf16[1,16,256,256]{3,2,1,0:T(8,128)(2,1)S(1)}, bf16[1,16,256,256]{3,2,1,0:T(8,128)(2,1)}, u32[]{:S(2)}) copy-start(bf16[1,16,256,256]{3,2,1,0:T(8,128)(2,1)} %param.15) | copy-start | bytes 6291460
  131.4 203.6 %all-gather.10.cloned.1.call-start = ((), (), s32[]{:S(2)}) async-start(), calls=%async_computation.2 | async-start | bytes 1179648 | tf_op jit(solution)/shard_map/all_gather | solution.py:56
  278.2 211.0 %all-gather.12.cloned.1.call-start = ((), (), s32[]{:S(2)}) async-start(), calls=%async_computation.3 | async-start | bytes 1179648 | tf_op jit(solution)/shard_map/all_gather | solution.py:56
  432.3 211.0 %all-gather.14.cloned.1.call-start = ((), (), s32[]{:S(2)}) async-start(), calls=%async_computation.4 | async-start | bytes 1179648 | tf_op jit(solution)/shard_map/all_gather | solution.py:56
  692.6 36.8 %collective-permute-start = (bf16[1,17,256,256]{2,3,1,0:T(8,128)(2,1)}, bf16[1,17,256,256]{2,3,1,0:T(8,128)(2,1)S(1)}, u32[]{:S(2)}, u32[]{:S(2)}) collective-permute-start(bf16[1,17,256,256]{2,3,1,0:T(8,128)(2,1)} %fusion.2), channel_id=1, source_target_pairs={{0,8},{8,16},{16,24},{1,9},{9,17},{17,25},{2,10},{10,18},{18,26},{... | collective-permute-start | bytes 6684680 | tf_op jit(solution)/shard_map/ppermute | solution.py:17
  709.8 29.1 %collective-permute-start.1 = (bf16[1,17,256,256]{3,2,1,0:T(8,128)(2,1)}, bf16[1,17,256,256]{3,2,1,0:T(8,128)(2,1)}, u32[]{:S(2)}, u32[]{:S(2)}) collective-permute-start(bf16[1,17,256,256]{3,2,1,0:T(8,128)(2,1)} %fusion.3), channel_id=1, source_target_pairs={{8,0},{16,8},{24,16},{9,1},{17,9},{25,17},{10,2},{18,10},{26,18},{... | collective-permute-start | bytes 6684680 | tf_op jit(solution)/shard_map/ppermute | solution.py:17
  729.4 1.4 copy-start.3
  734.4 4.4 copy-start.6
Sparse Core Ops, SparseCore 0:
  30.9 40.1 all-gather.5
  131.5 49.1 all-gather.7
  278.3 56.7 all-gather.9
  432.4 56.7 all-gather.11
  586.6 56.7 all-gather.13
where the time goes:
time: 752 us; the launch traced here: 750 us
  blocking collectives  321 us (43%)
  waiting for transfers between devices  268 us (36%)
  matrix products  51.5 us (7%)
  between operations  36.5 us (5%)
  local copies, waits for them, and re-layouts  36 us (5%)
  other arithmetic  22.6 us (3%)
  starting transfers between devices  14.6 us (2%)
    all_gather x5, waiting for transfers between devices, apply(): whole = lax.all_gather(rounded, 'blk', axis=0, tiled=True)  249 us
    psum x4, blocking collectives, on_device(): spread = lax.psum(total(correction, correction), 'blk')  61.7 us
    psum x4, blocking collectives, on_device(): rayleigh = lax.psum(total(state, image), 'blk')  61.5 us
    psum x4, blocking collectives, on_device(): lax.psum((total(state, pushed), total(direction, pushed)), 'blk')  60.9 us
    psum x4, blocking collectives, on_device(): newsq = lax.psum(total(state, state), 'blk')  59.4 us
    psum x4, blocking collectives, on_device(): correlation = lax.psum(total(state, correction), 'blk')  58.5 us
    dot_general x5, matrix products, apply(): jnp.einsum('qkij,qkjl->qil', middle, right_hop, preferred_element_type=jn...  23.5 us
    reduce_sum x16, other arithmetic, total(): return jnp.sum(first * second)  22.3 us
  transfers between devices with their start and end apart: 7, of which 7 were waited for; matrix products, arithmetic and copies ran while one was open for 3% of the time, Pallas kernels for 0%

commit v1 on v0

v1 whole, which is shorter than its diff:
```python
import functools
import math

import jax
import jax.numpy as jnp
from jax import lax
from jax.experimental import pallas as pl
from jax.experimental.pallas import tpu as pltpu
from jax.sharding import PartitionSpec as P

ITERS = 4
EPS = 1e-06
F32 = jnp.float32
BF16 = jnp.bfloat16
MESH = pl.DeviceIdType.MESH


def ring_order(count):
    depth = 4 if count % 4 == 0 else 2
    across = count // depth
    order = [z * across for z in range(depth)]
    for z in reversed(range(depth)):
        row = list(range(1, across))
        if (depth - 1 - z) % 2:
            row.reverse()
        order += [z * across + y for y in row]
    return order


def pick(table, index):
    value = jnp.int32(table[0])
    for place in range(1, len(table)):
        value = jnp.where(index == place, jnp.int32(table[place]), value)
    return value


def dot(first, second, contract=((1,), (0,))):
    return lax.dot_general(first, second, (contract, ((), ())), preferred_element_type=F32)


def kernel(
    group,
    segments,
    sizes_ref,
    partner_ref,
    start_ref,
    ldiag_ref,
    rdiag_ref,
    lcoup_ref,
    rcoup_ref,
    lhop_ref,
    rhop_ref,
    state_ref,
    energy_ref,
    lbound_ref,
    rbound_ref,
    left_ops,
    right_ops,
    field,
    middle,
    v_ref,
    h_ref,
    p_ref,
    q_ref,
    inverse_ref,
    sums,
    coup_out,
    coup_in,
    mix_left,
    mix_right,
    edge_out,
    edge_in,
    load_sem,
    ring_send,
    ring_recv,
    sum_send,
    sum_recv,
    coup_send,
    coup_recv,
    edge_send,
    edge_recv,
):
    seg = lax.axis_index("seg")
    me = lax.axis_index("blk")
    width = start_ref.shape[1]
    channels = lhop_ref.shape[1]
    half = width // 2
    has_next = seg < segments - 1
    has_prev = seg > 0

    loads = (
        pltpu.make_async_copy(lhop_ref.at[0], left_ops, load_sem.at[0]),
        pltpu.make_async_copy(rhop_ref.at[0], right_ops, load_sem.at[1]),
    )
    for load in loads:
        load.start()

    barrier = pltpu.get_barrier_semaphore()
    for step in range(1, group):
        pl.semaphore_signal(
            barrier, inc=1, device_id={"blk": lax.rem(me + step, group)}, device_id_type=MESH
        )

    @pl.when(has_next)
    def _():
        pl.semaphore_signal(barrier, inc=1, device_id={"seg": seg + 1}, device_id_type=MESH)

    @pl.when(has_prev)
    def _():
        pl.semaphore_signal(barrier, inc=1, device_id={"seg": seg - 1}, device_id_type=MESH)

    size = sizes_ref[0]
    rows = lax.broadcasted_iota(jnp.int32, (width, width), 0)
    cols = lax.broadcasted_iota(jnp.int32, (width, width), 1)
    on_diag = rows == cols
    left_line = jnp.sum(
        jnp.where(on_diag, ldiag_ref[0].astype(F32), 0.0), axis=1, keepdims=True
    )
    right_line = jnp.sum(
        jnp.where(on_diag, rdiag_ref[0].astype(F32), 0.0), axis=0, keepdims=True
    )
    inverse_ref[...] = 1.0 / (left_line + right_line)

    def masked(value):
        return jnp.where((rows < size) & (cols < size), value, 0.0)

    p_ref[...] = masked(start_ref[0])
    field[me] = p_ref[...].astype(BF16)
    coup_out[...] = jnp.zeros_like(coup_out)
    coup_out[0, 0:1, 0 : channels + 1] = lcoup_ref[...]
    coup_out[1, 0:1, 0 : channels + 1] = rcoup_ref[...]

    others = jnp.int32(group - 1) + has_next.astype(jnp.int32) + has_prev.astype(jnp.int32)
    pl.semaphore_wait(barrier, others)

    order = ring_order(group)
    place = [order.index(blk) for blk in range(group)]

    def along(step):
        return pick([order[(place[blk] + step) % group] for blk in range(group)], me)

    far = group // 2
    source = [[along(-1 - j) for j in range(far)], [along(1 + j) for j in range(far)]]
    target = [source[1][0], source[0][0]]
    lanes = [(0, 0), (1, 1), (0, 1), (1, 0)]

    def count(side, part):
        return far if side == part else far - 1

    def ring(side, part, j, slot):
        piece = field.at[slot, pl.ds(part * half, half), :]
        return pltpu.make_async_remote_copy(
            src_ref=piece,
            dst_ref=piece,
            send_sem=ring_send.at[side, part, j],
            recv_sem=ring_recv.at[side, part, j],
            device_id={"blk": target[side]},
            device_id_type=MESH,
        )

    def send_own():
        for side, part in lanes:
            ring(side, part, 0, me).start()

    def pass_on():
        for j in range(far):
            for side, part in lanes:
                if j < count(side, part):
                    ring(side, part, j, source[side][j]).wait_recv()
                    if j + 1 < count(side, part):
                        ring(side, part, j + 1, source[side][j]).start()

    def drain():
        for side, part in lanes:
            for j in range(count(side, part)):
                slot = me if j == 0 else source[side][j - 1]
                ring(side, part, j, slot).wait_send()

    def sum_copy(step):
        return pltpu.make_async_remote_copy(
            src_ref=sums.at[me],
            dst_ref=sums.at[me],
            send_sem=sum_send.at[step],
            recv_sem=sum_recv.at[step],
            device_id={"blk": lax.rem(me + step, group)},
            device_id_type=MESH,
        )

    def totals(products):
        for place_, (first, second) in enumerate(products):
            line = jnp.sum(first * second, axis=0, keepdims=True)
            short = line[:, 0:128]
            for begin in range(128, width, 128):
                short = short + line[:, begin : begin + 128]
            sums[me, place_ : place_ + 1, :] = short
        for step in range(1, group):
            sum_copy(step).start()
        for step in range(1, group):
            sum_copy(step).wait()
        whole = sums[0]
        for blk in range(1, group):
            whole = whole + sums[blk]
        whole = jnp.sum(whole, axis=1, keepdims=True)
        return [whole[i : i + 1, :] for i in range(len(products))]

    def own_terms():
        own = field[me]
        q_ref[...] = dot(ldiag_ref[0], own) + dot(own, rdiag_ref[0])

    def hop_terms():
        for k in range(channels):
            block = field[partner_ref[0, k]]
            middle[:, k * width : (k + 1) * width] = dot(left_ops[k], block).astype(BF16)
        q_ref[...] = masked(
            q_ref[...] + dot(middle[...], right_ops[...].reshape(channels * width, width))
        )

    def next_correction(rayleigh):
        p_ref[...] = (h_ref[...] - rayleigh * v_ref[...]) * inverse_ref[...]
        field[me] = p_ref[...].astype(BF16)

    def coup_copy(which):
        shift = -1 if which == 0 else 1
        return pltpu.make_async_remote_copy(
            src_ref=coup_out.at[which],
            dst_ref=coup_in.at[which],
            send_sem=coup_send.at[which],
            recv_sem=coup_recv.at[which],
            device_id={"seg": seg + shift},
            device_id_type=MESH,
        )

    def mix(which, diag_ref, ops, mixed):
        weights = coup_in[which]
        mixed_sum = weights[0:1, 0:1] * diag_ref[0].astype(F32)
        for k in range(channels):
            mixed_sum = mixed_sum + weights[0:1, k + 1 : k + 2] * ops[k].astype(F32)
        mixed[...] = mixed_sum.astype(BF16)

    send_own()

    @pl.when(has_prev)
    def _():
        coup_copy(0).start()

    @pl.when(has_next)
    def _():
        coup_copy(1).start()

    own_terms()
    for load in loads:
        load.wait()

    @pl.when(has_next)
    def _():
        coup_copy(0).wait_recv()
        mix(0, ldiag_ref, left_ops, mix_left)

    @pl.when(has_prev)
    def _():
        coup_copy(1).wait_recv()
        mix(1, rdiag_ref, right_ops, mix_right)

    pass_on()
    hop_terms()
    drain()
    p = p_ref[...]
    pp, pq = totals([(p, p), (p, q_ref[...])])
    scale = lax.rsqrt(pp + EPS)
    v_ref[...] = scale * p
    h_ref[...] = scale * q_ref[...]
    next_correction(scale * scale * pq)

    def iterate(_, lowest):
        send_own()
        own_terms()
        pass_on()
        hop_terms()
        drain()
        v, h, p, q = v_ref[...], h_ref[...], p_ref[...], q_ref[...]
        vv, vp, pp, vh, vq, ph, pq = totals(
            [(v, v), (v, p), (p, p), (v, h), (v, q), (p, h), (p, q)]
        )
        g = vp
        spread = jnp.maximum(pp - 2.0 * g * vp + g * g * vv, 0.0)
        unit = lax.rsqrt(spread + EPS)
        coupling = unit * (vq - g * vh)
        curvature = unit * unit * (pq - g * ph - g * vq + g * g * vh)
        bend = 0.5 * (curvature - vh)
        radius = jnp.sqrt(bend * bend + coupling * coupling)
        lowest = 0.5 * (vh + curvature) - radius
        alpha, beta = radius + bend, -coupling
        vu = unit * (vp - g * vv)
        uu = unit * unit * spread
        newsq = alpha * alpha * vv + 2.0 * alpha * beta * vu + beta * beta * uu
        scale = lax.rsqrt(newsq + EPS)
        with_p = scale * beta * unit
        with_v = scale * alpha - with_p * g
        v_ref[...] = with_v * v + with_p * p
        h_ref[...] = with_v * h + with_p * q
        rayleigh = with_v * with_v * vh + with_v * with_p * (vq + ph) + with_p * with_p * pq
        next_correction(rayleigh)
        return lowest

    lowest = lax.fori_loop(0, ITERS, iterate, jnp.zeros((1, 1), F32))
    energy_ref[...] = lowest
    state_ref[0] = v_ref[...]
    z = (v_ref[...] * (width * math.sqrt(group))).astype(BF16)

    def edge_copy(which):
        shift = 1 if which == 0 else -1
        return pltpu.make_async_remote_copy(
            src_ref=edge_out.at[which],
            dst_ref=edge_in.at[which],
            send_sem=edge_send.at[which],
            recv_sem=edge_recv.at[which],
            device_id={"seg": seg + shift},
            device_id_type=MESH,
        )

    @pl.when(has_next)
    def _():
        inner = dot(mix_left[...], z).astype(BF16)
        edge_out[0] = (dot(z, inner, ((0,), (0,))) * (1.0 / width)).astype(BF16)
        edge_copy(0).start()

    @pl.when(has_prev)
    def _():
        inner = dot(z, mix_right[...]).astype(BF16)
        edge_out[1] = (dot(inner, z, ((1,), (1,))) * (1.0 / width)).astype(BF16)
        edge_copy(1).start()

    @pl.when(has_prev)
    def _():
        coup_copy(0).wait_send()
        edge_copy(0).wait_recv()
        lbound_ref[0] = edge_in[0]
        edge_copy(1).wait_send()

    @pl.when(jnp.logical_not(has_prev))
    def _():
        lbound_ref[...] = jnp.zeros_like(lbound_ref)

    @pl.when(has_next)
    def _():
        coup_copy(1).wait_send()
        edge_copy(1).wait_recv()
        rbound_ref[0] = edge_in[1]
        edge_copy(0).wait_send()

    @pl.when(jnp.logical_not(has_next))
    def _():
        rbound_ref[...] = jnp.zeros_like(rbound_ref)


def on_device(
    group,
    segments,
    start_state,
    sector_sizes,
    partner,
    left_diag,
    right_diag,
    left_hop,
    right_hop,
    left_coupling,
    right_coupling,
):
    width = start_state.shape[1]
    channels = left_hop.shape[1]
    far = group // 2
    vmem = pl.BlockSpec(memory_space=pltpu.VMEM)
    smem = pl.BlockSpec(memory_space=pltpu.SMEM)
    hbm = pl.BlockSpec(memory_space=pl.ANY)
    square = (width, width)
    state, energy, left_boundary, right_boundary = pl.pallas_call(
        functools.partial(kernel, group, segments),
        out_shape=(
            jax.ShapeDtypeStruct((1,) + square, F32),
            jax.ShapeDtypeStruct((1, 1), F32),
            jax.ShapeDtypeStruct((1,) + square, BF16),
            jax.ShapeDtypeStruct((1,) + square, BF16),
        ),
        in_specs=[smem, smem, vmem, vmem, vmem, vmem, vmem, hbm, hbm],
        out_specs=(vmem, vmem, vmem, vmem),
        scratch_shapes=[
            pltpu.VMEM((channels,) + square, BF16),
            pltpu.VMEM((channels,) + square, BF16),
            pltpu.VMEM((group,) + square, BF16),
            pltpu.VMEM((width, channels * width), BF16),
            pltpu.VMEM(square, F32),
            pltpu.VMEM(square, F32),
            pltpu.VMEM(square, F32),
            pltpu.VMEM(square, F32),
            pltpu.VMEM(square, F32),
            pltpu.VMEM((group, 8, 128), F32),
            pltpu.VMEM((2, 8, 128), F32),
            pltpu.VMEM((2, 8, 128), F32),
            pltpu.VMEM(square, BF16),
            pltpu.VMEM(square, BF16),
            pltpu.VMEM((2,) + square, BF16),
            pltpu.VMEM((2,) + square, BF16),
            pltpu.SemaphoreType.DMA((2,)),
            pltpu.SemaphoreType.DMA((2, 2, far)),
            pltpu.SemaphoreType.DMA((2, 2, far)),
            pltpu.SemaphoreType.DMA((group,)),
            pltpu.SemaphoreType.DMA((group,)),
            pltpu.SemaphoreType.DMA((2,)),
            pltpu.SemaphoreType.DMA((2,)),
            pltpu.SemaphoreType.DMA((2,)),
            pltpu.SemaphoreType.DMA((2,)),
        ],
        compiler_params=pltpu.CompilerParams(
            collective_id=0, has_side_effects=True, vmem_limit_bytes=40 * 1024 * 1024
        ),
    )(
        sector_sizes,
        partner,
        start_state,
        left_diag,
        right_diag,
        left_coupling,
        right_coupling,
        left_hop,
        right_hop,
    )
    return state, jnp.reshape(energy, (1,)), left_boundary, right_boundary


def solution(mesh):
    block = P(("seg", "blk"), None, None)
    placed = (
        block,
        P(("seg", "blk")),
        P(("seg", "blk"), None),
        block,
        block,
        P(("seg", "blk"), None, None, None),
        P(("seg", "blk"), None, None, None),
        P("seg", None),
        P("seg", None),
    )
    return jax.shard_map(
        functools.partial(on_device, mesh.shape["blk"], mesh.shape["seg"]),
        mesh=mesh,
        in_specs=placed,
        out_specs=(block, P("seg"), block, block),
        check_vma=False,
    )
```

time: 752 us -> 126 us (0.17)
  blocking collectives: 321 us -> 0 us
  waiting for transfers between devices: 268 us -> 0 us
  Pallas kernels: 0 us -> 113 us
  matrix products: 51.5 us -> 0 us
  between operations: 36.5 us -> 3.12 us
  local copies, waits for them, and re-layouts: 36 us -> 9.91 us
  other arithmetic: 22.6 us -> 0 us
  starting transfers between devices: 14.6 us -> 0 us
    psum x21 -> x0, blocking collectives: 321 us -> none  [the longest x4 61.7 us: on_device(): spread = lax.psum(total(correction, correction), 'blk')]
    all_gather x5 -> x0, waiting for transfers between devices: 249 us -> none  [apply(): whole = lax.all_gather(rounded, 'blk', axis=0, tiled=True)]
    pallas_call x0 -> x1, Pallas kernels: none -> 113 us  [on_device(): pl.pallas_call(functools.partial(kernel, group, segments), out_shape=(jax...]
    dot_general x19 -> x0, matrix products: 51.5 us -> none  [the longest x5 23.5 us: apply(): jnp.einsum('qkij,qkjl->qil', middle, right_hop, preferred_element_type=jn...]
    reduce_sum x16 -> x0, other arithmetic: 22.3 us -> none  [total(): return jnp.sum(first * second)]
    gather x7 -> x0, local copies, waits for them, and re-layouts: 21.4 us -> none  [the longest x5 16.3 us: apply(): source = whole[partner]]
    ppermute x2 -> x0, waiting for transfers between devices: 18.5 us -> none  [passed_along(): lax.ppermute(value, axis, [(source, source + steps) for source in range(f...]
    ppermute x2 -> x0, starting transfers between devices: 14.3 us -> none  [passed_along(): lax.ppermute(value, axis, [(source, source + steps) for source in range(f...]
  transfers between devices with their start and end apart: 7 -> 0, of which waited for: 7 -> 0; matrix products, arithmetic and copies ran while one was open for 3% -> 0% of each run, Pallas kernels for 0% -> 0%
where the time goes in v1:
time: 126 us
  Pallas kernels  113 us (90%)
  local copies, waits for them, and re-layouts  9.91 us (8%)
  between operations  3.12 us (2%)
    pallas_call x1, Pallas kernels, on_device(): pl.pallas_call(functools.partial(kernel, group, segments), out_shape=(jax...  113 us
    unnamed x19, local copies, waits for them, and re-layouts  9.91 us

profile of v1, /device:TPU:1, one launch (start us, length us, event | category | flops | bytes accessed | tf_op | source)
XLA Modules:
  0.0 126.0 jit_solution(3058856235498431383)
XLA Ops:
  1.3 0.0 copy-start
  1.3 1.6 %copy-done = bf16[1,16,256,256]{3,2,1,0:T(8,128)(2,1)S(1)} copy-done((bf16[1,16,256,256]{3,2,1,0:T(8,128)(2,1)S(1)}, bf16[1,16,256,256]{3,2,1,0:T(8,128)(2,1)}, u32[]{:S(2)}) %copy-start) | copy-done | bytes 2097176
  2.9 0.0 copy-start.1
  2.9 1.6 %copy-done.1 = bf16[1,16,256,256]{3,2,1,0:T(8,128)(2,1)S(1)} copy-done((bf16[1,16,256,256]{3,2,1,0:T(8,128)(2,1)S(1)}, bf16[1,16,256,256]{3,2,1,0:T(8,128)(2,1)}, u32[]{:S(2)}) %copy-start.1) | copy-done | bytes 2097176
  4.5 0.0 copy-start.2
  4.5 0.9 copy-done.2
  5.4 0.0 copy-start.3
  5.4 0.9 copy-done.3
  6.3 0.0 copy-start.4
  6.3 0.9 copy-done.4
  7.2 0.0 copy-start.5
  7.2 0.7 copy-done.5
  7.9 0.0 copy-start.6
  7.9 0.7 copy-done.6
  8.5 0.0 copy-start.7
  8.5 0.7 copy-done.7
  9.2 112.9 %shard_map.120 = (f32[1,256,256]{2,1,0:T(8,128)S(1)}, f32[1,1]{1,0:T(1,128)}, bf16[1,256,256]{2,1,0:T(8,128)(2,1)S(1)}, bf16[1,256,256]{2,1,0:T(8,128)(2,1)S(1)}) custom-call(s32[1]{0:T(128)S(6)} %copy.17.sizes_ref, s32[1,16]{1,0:T(1,128)S(1)} %copy-done.5, f32[1,256,256]{2,1,0:T(8,128)S(1)} %copy-done.2, bf16[1,256,256]{2,1,0:T(8,128)(2,1)S(1)} %copy-done.3, ...), custom_call_target="tpu_custom_call" | custom-call | tf_op jit(solution)/shard_map/pallas_call | solution.py:376
  122.1 0.7 copy.18
  123.5 0.7 copy.20
  124.2 0.7 copy.21
Async XLA Ops:
  1.3 1.6 %copy-start = (bf16[1,16,256,256]{3,2,1,0:T(8,128)(2,1)S(1)}, bf16[1,16,256,256]{3,2,1,0:T(8,128)(2,1)}, u32[]{:S(2)}) copy-start(bf16[1,16,256,256]{3,2,1,0:T(8,128)(2,1)} %lhop_ref.1) | copy-start | bytes 6291460
  2.9 1.6 %copy-start.1 = (bf16[1,16,256,256]{3,2,1,0:T(8,128)(2,1)S(1)}, bf16[1,16,256,256]{3,2,1,0:T(8,128)(2,1)}, u32[]{:S(2)}) copy-start(bf16[1,16,256,256]{3,2,1,0:T(8,128)(2,1)} %rhop_ref.1) | copy-start | bytes 6291460
  4.5 0.9 copy-start.2
  5.4 0.9 copy-start.3
  6.3 0.9 copy-start.4
  7.2 0.7 copy-start.5
  7.9 0.7 copy-start.6
  8.5 0.7 copy-start.7

commit v2 on v1

--- a/solution.py
+++ b/solution.py
@@ -10,6 +10,7 @@
 
 ITERS = 4
 EPS = 1e-06
+PARTS = 4
 F32 = jnp.float32
 BF16 = jnp.bfloat16
 MESH = pl.DeviceIdType.MESH
@@ -41,6 +42,19 @@
 def kernel(
     group,
     segments,
+    sizes_in,
+    partner_in,
+    start_in,
+    ldiag_in,
+    rdiag_in,
+    lcoup_in,
+    rcoup_in,
+    lhop_in,
+    rhop_in,
+    state_ref,
+    energy_ref,
+    lbound_ref,
+    rbound_ref,
     sizes_ref,
     partner_ref,
     start_ref,
@@ -48,12 +62,6 @@
     rdiag_ref,
     lcoup_ref,
     rcoup_ref,
-    lhop_ref,
-    rhop_ref,
-    state_ref,
-    energy_ref,
-    lbound_ref,
-    rbound_ref,
     left_ops,
     right_ops,
     field,
@@ -83,15 +91,26 @@
     seg = lax.axis_index("seg")
     me = lax.axis_index("blk")
     width = start_ref.shape[1]
-    channels = lhop_ref.shape[1]
-    half = width // 2
+    channels = lhop_in.shape[1]
+    half = width // PARTS
     has_next = seg < segments - 1
     has_prev = seg > 0
 
-    loads = (
-        pltpu.make_async_copy(lhop_ref.at[0], left_ops, load_sem.at[0]),
-        pltpu.make_async_copy(rhop_ref.at[0], right_ops, load_sem.at[1]),
-    )
+    pairs = (
+        (start_in, start_ref),
+        (sizes_in, sizes_ref),
+        (partner_in, partner_ref),
+        (ldiag_in, ldiag_ref),
+        (rdiag_in, rdiag_ref),
+        (lcoup_in, lcoup_ref),
+        (rcoup_in, rcoup_ref),
+        (lhop_in.at[0], left_ops),
+        (rhop_in.at[0], right_ops),
+    )
+    loads = [
+        pltpu.make_async_copy(origin, held, load_sem.at[i])
+        for i, (origin, held) in enumerate(pairs)
+    ]
     for load in loads:
         load.start()
 
@@ -109,6 +128,8 @@
     def _():
         pl.semaphore_signal(barrier, inc=1, device_id={"seg": seg - 1}, device_id_type=MESH)
 
+    for load in loads[:7]:
+        load.wait()
     size = sizes_ref[0]
     rows = lax.broadcasted_iota(jnp.int32, (width, width), 0)
     cols = lax.broadcasted_iota(jnp.int32, (width, width), 1)
@@ -142,10 +163,11 @@
     far = group // 2
     source = [[along(-1 - j) for j in range(far)], [along(1 + j) for j in range(far)]]
     target = [source[1][0], source[0][0]]
-    lanes = [(0, 0), (1, 1), (0, 1), (1, 0)]
+    first = [lane for i in range(PARTS // 2) for lane in ((0, i), (1, PARTS // 2 + i))]
+    lanes = first + [(1 - side, part) for side, part in first]
 
     def count(side, part):
-        return far if side == part else far - 1
+        return far if side == part // (PARTS // 2) else far - 1
 
     def ring(side, part, j, slot):
         piece = field.at[slot, pl.ds(part * half, half), :]
@@ -187,12 +209,15 @@
         )
 
     def totals(products):
+        lane = lax.broadcasted_iota(jnp.int32, (1, 128), 1)
+        row = jnp.zeros((1, 128), F32)
         for place_, (first, second) in enumerate(products):
             line = jnp.sum(first * second, axis=0, keepdims=True)
             short = line[:, 0:128]
             for begin in range(128, width, 128):
                 short = short + line[:, begin : begin + 128]
-            sums[me, place_ : place_ + 1, :] = short
+            row = row + jnp.where(lane == place_, jnp.sum(short, axis=1, keepdims=True), 0.0)
+        sums[me] = row
         for step in range(1, group):
             sum_copy(step).start()
         for step in range(1, group):
@@ -200,8 +225,7 @@
         whole = sums[0]
         for blk in range(1, group):
             whole = whole + sums[blk]
-        whole = jnp.sum(whole, axis=1, keepdims=True)
-        return [whole[i : i + 1, :] for i in range(len(products))]
+        return [whole[:, i : i + 1] for i in range(len(products))]
 
     def own_terms():
         own = field[me]
@@ -248,7 +272,7 @@
         coup_copy(1).start()
 
     own_terms()
-    for load in loads:
+    for load in loads[7:]:
         load.wait()
 
     @pl.when(has_next)
@@ -370,7 +394,6 @@
     channels = left_hop.shape[1]
     far = group // 2
     vmem = pl.BlockSpec(memory_space=pltpu.VMEM)
-    smem = pl.BlockSpec(memory_space=pltpu.SMEM)
     hbm = pl.BlockSpec(memory_space=pl.ANY)
     square = (width, width)
     state, energy, left_boundary, right_boundary = pl.pallas_call(
@@ -381,9 +404,16 @@
             jax.ShapeDtypeStruct((1,) + square, BF16),
             jax.ShapeDtypeStruct((1,) + square, BF16),
         ),
-        in_specs=[smem, smem, vmem, vmem, vmem, vmem, vmem, hbm, hbm],
+        in_specs=[hbm] * 9,
         out_specs=(vmem, vmem, vmem, vmem),
         scratch_shapes=[
+            pltpu.SMEM(sector_sizes.shape, jnp.int32),
+            pltpu.SMEM(partner.shape, jnp.int32),
+            pltpu.VMEM((1,) + square, F32),
+            pltpu.VMEM((1,) + square, BF16),
+            pltpu.VMEM((1,) + square, BF16),
+            pltpu.VMEM(left_coupling.shape, F32),
+            pltpu.VMEM(right_coupling.shape, F32),
             pltpu.VMEM((channels,) + square, BF16),
             pltpu.VMEM((channels,) + square, BF16),
             pltpu.VMEM((group,) + square, BF16),
@@ -393,16 +423,16 @@
             pltpu.VMEM(square, F32),
             pltpu.VMEM(square, F32),
             pltpu.VMEM(square, F32),
-            pltpu.VMEM((group, 8, 128), F32),
+            pltpu.VMEM((group, 1, 128), F32),
             pltpu.VMEM((2, 8, 128), F32),
             pltpu.VMEM((2, 8, 128), F32),
             pltpu.VMEM(square, BF16),
             pltpu.VMEM(square, BF16),
             pltpu.VMEM((2,) + square, BF16),
             pltpu.VMEM((2,) + square, BF16),
-            pltpu.SemaphoreType.DMA((2,)),
-            pltpu.SemaphoreType.DMA((2, 2, far)),
-            pltpu.SemaphoreType.DMA((2, 2, far)),
+            pltpu.SemaphoreType.DMA((9,)),
+            pltpu.SemaphoreType.DMA((2, PARTS, far)),
+            pltpu.SemaphoreType.DMA((2, PARTS, far)),
             pltpu.SemaphoreType.DMA((group,)),
             pltpu.SemaphoreType.DMA((group,)),
             pltpu.SemaphoreType.DMA((2,)),
@@ -411,7 +441,7 @@
             pltpu.SemaphoreType.DMA((2,)),
         ],
         compiler_params=pltpu.CompilerParams(
-            collective_id=0, has_side_effects=True, vmem_limit_bytes=40 * 1024 * 1024
+            collective_id=0, has_side_effects=True, vmem_limit_bytes=60 * 1024 * 1024
         ),
     )(
         sector_sizes,

time: 126 us -> 113 us (0.90)
  Pallas kernels: 113 us -> 105 us
  local copies, waits for them, and re-layouts: 9.91 us -> 4.81 us
    pallas_call x1, Pallas kernels: 113 us -> 105 us  [on_device(): pl.pallas_call(functools.partial(kernel, group, segments), out_shape=(jax...]
    unnamed x19 -> x3, local copies, waits for them, and re-layouts: 9.91 us -> 4.81 us
where the time goes in v2:
time: 113 us
  Pallas kernels  105 us (93%)
  local copies, waits for them, and re-layouts  4.81 us (4%)
  between operations  2.99 us (3%)
    pallas_call x1, Pallas kernels, on_device(): pl.pallas_call(functools.partial(kernel, group, segments), out_shape=(jax...  105 us
    unnamed x3, local copies, waits for them, and re-layouts  4.81 us

profile of v2, /device:TPU:1, one launch (start us, length us, event | category | flops | bytes accessed | tf_op | source)
XLA Modules:
  0.0 113.1 jit_solution(860716968142316802)
XLA Ops:
  1.3 105.3 %shard_map.120 = (f32[1,256,256]{2,1,0:T(8,128)}, f32[1,1]{1,0:T(1,128)}, bf16[1,256,256]{2,1,0:T(8,128)(2,1)}, bf16[1,256,256]{2,1,0:T(8,128)(2,1)}) custom-call(s32[1]{0:T(128)S(6)} %copy.17.sizes_in, s32[1,16]{1,0:T(1,128)} %partner_in.1, f32[1,256,256]{2,1,0:T(8,128)} %start_in.1, bf16[1,256,256]{2,1,0:T(8,128)(2,1)} %ldiag_in.1, ...), custom_call_target="tpu_custom_call" | custom-call | tf_op jit(solution)/shard_map/pallas_call | solution.py:399
  106.6 1.7 %copy.18 = f32[1,256,256]{2,1,0:T(8,128)} copy(f32[1,256,256]{2,1,0:T(8,128)} %get-tuple-element.16) | data formatting | bytes 524288
  108.8 1.6 %copy.20 = bf16[1,256,256]{2,1,0:T(8,128)(2,1)} copy(bf16[1,256,256]{2,1,0:T(8,128)(2,1)} %get-tuple-element.18) | data formatting | bytes 262144
  110.4 1.6 %copy.21 = bf16[1,256,256]{2,1,0:T(8,128)(2,1)} copy(bf16[1,256,256]{2,1,0:T(8,128)(2,1)} %get-tuple-element.19) | data formatting | bytes 262144
